TPU v7x, 128 devices: a whole 4x4x4 slice. The times are simulated.
128 devices in a mesh: dp: 8 (over y, core), ctx: 16 (over x, z).
Axes of the slice: x: 4, y: 4, z: 4, core: 2. Of those that a mesh axis runs over, the one named last changes fastest.
Arguments:
- queries: bfloat16 [8, 4096, 4096], P('dp', 'ctx'), may hold values from -6 to 6
- keys_in: bfloat16 [8, 4096, 4096], P('dp', 'ctx'), may hold values from -6 to 6
- values_in: bfloat16 [8, 4096, 4096], P('dp', 'ctx'), may hold values from -6 to 6
- filters: float32 [4096, 4096], P('ctx'), may hold values from -0.09375 to 0.09375
- skip_gain: float32 [4096], replicated, may hold values from -4 to 4
- out_weight: bfloat16 [4096, 4096], P(None, ('dp', 'ctx')), may hold values from -0.09375 to 0.09375
Outputs:
- projected: bfloat16 [8, 4096, 4096], P('dp', 'ctx')
All inputs are finite; a program needn't handle non-finite values.
Results may differ from a plain program's by a relative error of at most 0.0064.
Values may be sent and summed in bfloat16 or wider, within the bound.
No kernel may reach another device: no remote copies, remote signals or barrier semaphores. Data moves between devices by JAX's collectives and lax.ppermute only.
A program may use at most 256 MiB of HBM per device.

v0:
```python
import math
import jax
import jax.numpy as jnp
from jax import lax
from jax.sharding import PartitionSpec as P


def angles(count_rows, count_cols, period):
    index = (
        jnp.arange(count_rows, dtype=jnp.int32)[:, None]
        * jnp.arange(count_cols, dtype=jnp.int32)[None, :]
        % period
    )
    theta = index.astype(jnp.float32) * (2.0 * math.pi / period)
    return (jnp.cos(theta), jnp.sin(theta))


def close_einsum(form, left, right):
    return jnp.einsum(form, left, right, precision=lax.Precision.HIGH)


def split_einsum(form, table, signal):
    table_high = lax.optimization_barrier(table.astype(jnp.bfloat16))
    table_low = (table - table_high.astype(jnp.float32)).astype(jnp.bfloat16)
    first_part = jnp.einsum(form, table_high, signal, preferred_element_type=jnp.float32)
    return first_part + jnp.einsum(form, table_low, signal, preferred_element_type=jnp.float32)


def forward(signal):
    half = signal.shape[1]
    full = 2 * half
    outer_cos, outer_sin = angles(full, half, full)
    twist_cos, twist_sin = angles(full, 128, full * 128)
    inner_cos, inner_sin = angles(128, 128, 128)
    twist_cos = twist_cos[:, :, None]
    twist_sin = twist_sin[:, :, None]
    if signal.dtype == jnp.bfloat16:
        first_re = split_einsum("kn,snbc->skbc", outer_cos, signal)
        first_im = -split_einsum("kn,snbc->skbc", outer_sin, signal)
    else:
        first_re = close_einsum("kn,snbc->skbc", outer_cos, signal)
        first_im = -close_einsum("kn,snbc->skbc", outer_sin, signal)
    middle_re = first_re * twist_cos + first_im * twist_sin
    middle_im = first_im * twist_cos - first_re * twist_sin
    spec_re = close_einsum("hb,skbc->skhc", inner_cos, middle_re) + close_einsum(
        "hb,skbc->skhc", inner_sin, middle_im
    )
    spec_im = close_einsum("hb,skbc->skhc", inner_cos, middle_im) - close_einsum(
        "hb,skbc->skhc", inner_sin, middle_re
    )
    return (spec_re, spec_im)


def inverse(spec_re, spec_im):
    full = spec_re.shape[1]
    half = full // 2
    outer_cos, outer_sin = angles(full, half, full)
    twist_cos, twist_sin = angles(full, 128, full * 128)
    inner_cos, inner_sin = angles(128, 128, 128)
    twist_cos = twist_cos[:, :, None]
    twist_sin = twist_sin[:, :, None]
    back_re = close_einsum("hb,skhc->skbc", inner_cos, spec_re) - close_einsum(
        "hb,skhc->skbc", inner_sin, spec_im
    )
    back_im = close_einsum("hb,skhc->skbc", inner_cos, spec_im) + close_einsum(
        "hb,skhc->skbc", inner_sin, spec_re
    )
    turned_re = back_re * twist_cos - back_im * twist_sin
    turned_im = back_im * twist_cos + back_re * twist_sin
    result = close_einsum("kn,skbc->snbc", outer_cos, turned_re) - close_einsum(
        "kn,skbc->snbc", outer_sin, turned_im
    )
    return result * (1.0 / (full * 128))


def on_device(queries, keys_in, values_in, filters, skip_gain, out_weight):
    product = (keys_in.astype(jnp.float32) * values_in.astype(jnp.float32)).astype(jnp.bfloat16)
    channels = filters.shape[0]
    length = filters.shape[1]
    half = length // 128
    response = filters.T.reshape(1, half, 128, channels)
    filt_re, filt_im = forward(response)
    local_skip = lax.dynamic_slice_in_dim(skip_gain, lax.axis_index("ctx") * channels, channels)
    piece = lax.all_to_all(product, "ctx", split_axis=2, concat_axis=1, tiled=True)
    count = piece.shape[0]
    signal = piece.astype(jnp.float32)
    spec_re, spec_im = forward(piece.reshape(count, half, 128, channels))
    prod_re = spec_re * filt_re - spec_im * filt_im
    prod_im = spec_re * filt_im + spec_im * filt_re
    causal = inverse(prod_re, prod_im).reshape(count, length, channels)
    mixed = (causal + local_skip[None, None, :] * signal).astype(jnp.bfloat16)
    returned = lax.all_to_all(mixed, "ctx", split_axis=1, concat_axis=2, tiled=True)
    gated = (queries.astype(jnp.float32) * returned.astype(jnp.float32)).astype(jnp.bfloat16)
    seq_count, tok_count, width = gated.shape
    tok_rows = gated.reshape(seq_count * tok_count, width)
    result = jnp.dot(
        tok_rows,
        lax.all_gather(out_weight, ("dp", "ctx"), axis=1, tiled=True),
        preferred_element_type=jnp.float32,
    ).astype(jnp.bfloat16)
    return result.reshape(seq_count, tok_count, result.shape[1])


def solution(mesh):
    in_specs = (
        P("dp", "ctx", None),
        P("dp", "ctx", None),
        P("dp", "ctx", None),
        P("ctx", None),
        P(),
        P(None, ("dp", "ctx")),
    )
    out_specs = P("dp", "ctx", None)
    return jax.shard_map(
        on_device, mesh=mesh, in_specs=in_specs, out_specs=out_specs, check_vma=False
    )
```

profile of v0, /device:TPU:0, one launch (start us, length us, event | category | flops | bytes accessed | tf_op | source)
XLA Modules:
  0.0 455.0 jit_solution(194958502813728175)
XLA Ops:
  10.3 7.3 %copy.93 = bf16[1,256,4096]{1,0,2:T(2,128)(2,1)} copy(bf16[1,256,4096]{2,1,0:T(8,128)(2,1)S(1)} %multiply_convert_fusion) | data formatting | bytes 4194304 | tf_op jit(solution)/shard_map/convert_element_type | solution.py:77
  18.1 21.6 %reduce = bf16[4096,256]{1,0:T(8,128)(2,1)S(1)} reduce(bf16[4096,1,256]{2,1,0:T(2,128)(2,1)} %bitcast.223, bf16[]{:T(256)} %broadcast.280), dimensions={1}, to_apply=%bitcast.182.reduce_sub_computation | reduce | bytes 4194306
  41.7 8.2 %all-to-all-start = ((bf16[16,2,32768]{2,1,0:T(2,128)(2,1)}), bf16[16,2,32768]{2,1,0:T(2,128)(2,1)S(1)}, u32[]{:S(2)}, u32[]{:S(2)}) async-start(bf16[16,2,32768]{2,1,0:T(2,128)(2,1)} %reshape.237), calls=%async_computation | async-start | bytes 4194304 | tf_op jit(solution)/shard_map/all_to_all | solution.py:84
  62.6 9.0 %fusion.82 = f32[64,128,256]{2,0,1:T(8,128)} fusion(f32[32,128,256]{2,0,1:T(8,128)} %copy.103), kind=kOutput, calls=%fused_computation.100 | convolution fusion | flops 402681856 | bytes 12582912 | tf_op jit(solution)/shard_map/kn,snbc->skbc/dot_general | solution.py:19
  77.6 9.1 %all-to-all-done = bf16[16,2,32768]{2,1,0:T(2,128)(2,1)S(1)} async-done(((bf16[16,2,32768]{2,1,0:T(2,128)(2,1)}), bf16[16,2,32768]{2,1,0:T(2,128)(2,1)S(1)}, u32[]{:S(2)}, u32[]{:S(2)}) %all-to-all-start) | async-done | bytes 2097184 | tf_op jit(solution)/shard_map/all_to_all | solution.py:84
  86.8 6.8 %reshape.238 = bf16[4096,1,256]{2,1,0:T(2,128)(2,1)} reshape(bf16[16,2,32768]{2,1,0:T(2,128)(2,1)S(1)} %all-to-all-done) | data formatting | bytes 4194304
  117.3 23.8 %fusion.17 = (f32[64,128,256]{2,0,1:T(8,128)}, f32[64,128,256]{2,0,1:T(8,128)}, f32[64,128,256]{2,0,1:T(8,128)}, f32[64,128,256]{2,0,1:T(8,128)}) fusion(f32[128,256,64]{1,2,0:T(8,128)} %add_negate_fusion, f32[64,128]{0,1:T(8,128)S(1)} %copy.100, f32[64,128]{0,1:T(8,128)S(1)} %copy.97, f32[128,256,64]{1,2,0:T(8,128)} %fusion.28, ...), kind=kOutput, calls=%fused_computation.27 | convolution fusion | flops 163577856 | bytes 69275648 | tf_op jit(solution)/shard_map/kn,snbc->skbc/dot_general | solution.py:25
  141.1 9.3 %copy.105 = f32[64,128,256]{1,2,0:T(8,128)} copy(f32[64,128,256]{2,0,1:T(8,128)} %get-tuple-element.14) | data formatting | bytes 16777216 | tf_op jit(solution)/shard_map/reshape.26
  150.4 9.3 %copy.101 = f32[64,128,256]{1,2,0:T(8,128)} copy(f32[64,128,256]{2,0,1:T(8,128)} %get-tuple-element.9) | data formatting | bytes 16777216 | tf_op jit(solution)/shard_map/reshape.16
  159.7 9.3 %copy.106 = f32[64,128,256]{1,2,0:T(8,128)} copy(f32[64,128,256]{2,0,1:T(8,128)} %get-tuple-element.13) | data formatting | bytes 16777216 | tf_op jit(solution)/shard_map/reshape.28
  168.9 9.3 %copy.102 = f32[64,128,256]{1,2,0:T(8,128)} copy(f32[64,128,256]{2,0,1:T(8,128)} %get-tuple-element.10) | data formatting | bytes 16777216 | tf_op jit(solution)/shard_map/reshape.20
  178.2 8.7 %fusion.43 = f32[64,256,128]{2,1,0:T(8,128)} fusion(f32[64,128,256]{1,2,0:T(8,128)} %copy.102), kind=kOutput, calls=%fused_computation.67 | convolution fusion | flops 1610842112 | bytes 16777216 | tf_op jit(solution)/shard_map/hb,skbc->skhc/dot_general | solution.py:19
  186.9 6.6 %fusion.49 = f32[64,256,128]{2,1,0:T(8,128)} fusion(f32[64,128,256]{1,2,0:T(8,128)S(1)} %copy-done.1), kind=kOutput, calls=%fused_computation.73 | convolution fusion | flops 1610842112 | bytes 16777216 | tf_op jit(solution)/shard_map/hb,skbc->skhc/dot_general | solution.py:19
  218.0 6.3 %fusion.41 = f32[64,256,128]{2,1,0:T(8,128)} fusion(f32[64,128,256]{1,2,0:T(8,128)S(1)} %bitcast.210), kind=kOutput, calls=%fused_computation.65 | convolution fusion | flops 1610842112 | bytes 16777216 | tf_op jit(solution)/shard_map/hb,skbc->skhc/dot_general | solution.py:19
  224.3 29.1 %multiply_subtract_fusion = (f32[64,256,128]{2,1,0:T(8,128)}, f32[64,256,128]{2,1,0:T(8,128)}) fusion(f32[64,256,128]{2,1,0:T(8,128)} %fusion.37, f32[64,256,128]{2,1,0:T(8,128)} %fusion.49, f32[64,256,128]{2,1,0:T(8,128)} %fusion.39, f32[64,256,128]{2,1,0:T(8,128)} %fusion.51, f32[64,256,128]{2,1,0:T(8,128)} %fusion.41, f32[64,256,128]{2,1,0:T(8,128)} %fusion.53, ...), kind=kOutput, calls=%fused_computation.33 | convolution fusion | flops 1631813632 | bytes 83886080 | tf_op jit(solution)/shard_map/hb,skbc->skhc/dot_general | solution.py:19
  253.4 8.7 %fusion.4 = f32[64,256,128]{2,1,0:T(8,128)} fusion(f32[64,256,128]{2,1,0:T(8,128)} %get-tuple-element.5), kind=kOutput, calls=%fused_computation.6 | convolution fusion | flops 1610842112 | bytes 16777216 | tf_op jit(solution)/shard_map/hb,skhc->skbc/dot_general | solution.py:19
  274.3 19.6 %fusion.3 = (f32[64,128,256]{1,2,0:T(8,128)}, f32[64,128,256]{1,2,0:T(8,128)}) fusion(f32[64,128]{1,0:T(8,128)S(1)} %get-tuple-element.15, f32[64,128]{1,0:T(8,128)S(1)} %get-tuple-element.16, f32[64,256,128]{2,1,0:T(8,128)} %fusion.8, f32[64,256,128]{2,1,0:T(8,128)} %fusion.4, f32[64,256,128]{2,1,0:T(8,128)} %fusion.6, f32[64,256,128]{2,1,0:T(8,128)} %get-tuple-element.6), kind=kOutput, calls=%fused_computation.5 | convolution fusion | flops 1627619328 | bytes 50397184 | tf_op jit(solution)/shard_map/hb,skhc->skbc/dot_general | solution.py:19
  293.8 9.2 %copy.111 = f32[64,128,256]{2,0,1:T(8,128)} copy(f32[64,128,256]{1,2,0:T(8,128)} %get-tuple-element.8) | data formatting | bytes 16777216 | tf_op jit(solution)/shard_map/reshape.46
  303.0 9.2 %copy.112 = f32[64,128,256]{2,0,1:T(8,128)} copy(f32[64,128,256]{1,2,0:T(8,128)} %get-tuple-element.7) | data formatting | bytes 16777216 | tf_op jit(solution)/shard_map/reshape.48
  324.8 25.3 %copy.131 = bf16[1,4096,256]{2,0,1:T(2,128)(2,1)} copy(bf16[1,4096,256]{2,1,0:T(8,128)(2,1)S(1)} %fusion.23) | data formatting | bytes 4194304 | tf_op jit(solution)/shard_map/convert_element_type | solution.py:91
  350.1 21.6 %reduce.1 = bf16[4096,256]{1,0:T(8,128)(2,1)S(1)} reduce(bf16[4096,1,256]{2,1,0:T(2,128)(2,1)} %bitcast.224, bf16[]{:T(256)} %broadcast.280), dimensions={1}, to_apply=%bitcast.208.reduce_sub_computation | reduce | bytes 4194306
  383.8 25.9 %all-to-all-done.1 = bf16[16,2,32768]{2,1,0:T(2,128)(2,1)S(1)} async-done(((bf16[16,2,32768]{2,1,0:T(2,128)(2,1)}), bf16[16,2,32768]{2,1,0:T(2,128)(2,1)S(1)}, u32[]{:S(2)}, u32[]{:S(2)}) %all-to-all-start.1) | async-done | bytes 2097184 | tf_op jit(solution)/shard_map/all_to_all | solution.py:92
  409.6 6.8 %reshape.240 = bf16[4096,1,256]{2,1,0:T(2,128)(2,1)} reshape(bf16[16,2,32768]{2,1,0:T(2,128)(2,1)S(1)} %all-to-all-done.1) | data formatting | bytes 4194304
  430.8 16.9 %fusion.20 = bf16[1,256,4096]{2,1,0:T(8,128)(2,1)} fusion(bf16[4096,4096]{0,1:T(8,128)(2,1)} %all-gather.2.cloned.1.call-done, bf16[1,256,4096]{1,2,0:T(8,128)(2,1)} %fusion.21), kind=kOutput, calls=%fused_computation.36 | convolution fusion | flops 8590983168 | bytes 37748736 | tf_op jit(solution)/shard_map/dot_general | solution.py:96
  (72 shorter events, 124.4 us)
Async XLA Ops:
  6.5 424.2 %all-gather.2.cloned.1.call-start = ((), (), s32[]{:S(2)}) async-start(), calls=%async_computation.2 | async-start | bytes 33816576 | tf_op jit(solution)/shard_map/all_gather | solution.py:98
  41.7 45.0 %all-to-all-start = ((bf16[16,2,32768]{2,1,0:T(2,128)(2,1)}), bf16[16,2,32768]{2,1,0:T(2,128)(2,1)S(1)}, u32[]{:S(2)}, u32[]{:S(2)}) async-start(bf16[16,2,32768]{2,1,0:T(2,128)(2,1)} %reshape.237), calls=%async_computation | async-start | bytes 4194304 | tf_op jit(solution)/shard_map/all_to_all | solution.py:84
  61.1 10.5 %copy-start.2 = (f32[32,128,256]{2,0,1:T(8,128)S(1)}, f32[32,128,256]{2,0,1:T(8,128)}, u32[]{:S(2)}) copy-start(f32[32,128,256]{2,0,1:T(8,128)} %copy.103) | copy-start | bytes 12582916
  178.2 8.7 %copy-start.1 = (f32[64,128,256]{1,2,0:T(8,128)S(1)}, f32[64,128,256]{1,2,0:T(8,128)}, u32[]{:S(2)}) copy-start(f32[64,128,256]{1,2,0:T(8,128)} %copy.102) | copy-start | bytes 25165828
  178.2 15.2 %slice-start.6 = ((s8[8388608]{0:T(1024)(128)(4,1)}), s8[4194304]{0:T(1024)(128)(4,1)S(1)}, s32[]{:S(2)}) async-start(s8[8388608]{0:T(1024)(128)(4,1)} %bitcast.215), calls=%async_computation.9 | async-start | bytes 8388608
  186.9 6.6 %slice-start.7 = ((s8[8388608]{0:T(1024)(128)(4,1)}), s8[4194304]{0:T(1024)(128)(4,1)S(1)}, s32[]{:S(2)}) async-start(s8[8388608]{0:T(1024)(128)(4,1)} %bitcast.215), calls=%async_computation.10 | async-start | bytes 8388608
  193.4 12.3 %slice-start.4 = ((s8[8388608]{0:T(1024)(128)(4,1)}), s8[4194304]{0:T(1024)(128)(4,1)S(1)}, s32[]{:S(2)}) async-start(s8[8388608]{0:T(1024)(128)(4,1)} %bitcast.213), calls=%async_computation.7 | async-start | bytes 8388608
  199.6 6.1 %slice-start.5 = ((s8[8388608]{0:T(1024)(128)(4,1)}), s8[4194304]{0:T(1024)(128)(4,1)S(1)}, s32[]{:S(2)}) async-start(s8[8388608]{0:T(1024)(128)(4,1)} %bitcast.213), calls=%async_computation.8 | async-start | bytes 8388608
  205.7 12.2 %slice-start = ((s8[8388608]{0:T(1024)(128)(4,1)}), s8[4194304]{0:T(1024)(128)(4,1)S(1)}, s32[]{:S(2)}) async-start(s8[8388608]{0:T(1024)(128)(4,1)} %bitcast.209), calls=%async_computation.3 | async-start | bytes 8388608
  211.9 6.1 %slice-start.1 = ((s8[8388608]{0:T(1024)(128)(4,1)}), s8[4194304]{0:T(1024)(128)(4,1)S(1)}, s32[]{:S(2)}) async-start(s8[8388608]{0:T(1024)(128)(4,1)} %bitcast.209), calls=%async_computation.4 | async-start | bytes 8388608
  253.4 8.7 %copy-start = (f32[64,256,128]{2,1,0:T(8,128)S(1)}, f32[64,256,128]{2,1,0:T(8,128)}, u32[]{:S(2)}) copy-start(f32[64,256,128]{2,1,0:T(8,128)} %get-tuple-element.5) | copy-start | bytes 25165828
  253.4 14.8 %slice-start.2 = ((s8[8388608]{0:T(1024)(128)(4,1)}), s8[4194304]{0:T(1024)(128)(4,1)S(1)}, s32[]{:S(2)}) async-start(s8[8388608]{0:T(1024)(128)(4,1)} %bitcast.211), calls=%async_computation.5 | async-start | bytes 8388608
  262.0 6.1 %slice-start.3 = ((s8[8388608]{0:T(1024)(128)(4,1)}), s8[4194304]{0:T(1024)(128)(4,1)S(1)}, s32[]{:S(2)}) async-start(s8[8388608]{0:T(1024)(128)(4,1)} %bitcast.211), calls=%async_computation.6 | async-start | bytes 8388608
  312.2 5.8 %copy-start.3 = (f32[64,128,256]{2,0,1:T(8,128)S(1)}, f32[64,128,256]{2,0,1:T(8,128)}, u32[]{:S(2)}) copy-start(f32[64,128,256]{2,0,1:T(8,128)} %copy.112) | copy-start | bytes 25165828
  321.1 2.5 copy-start.4
  321.1 2.5 copy-start.6
  373.6 36.0 %all-to-all-start.1 = ((bf16[16,2,32768]{2,1,0:T(2,128)(2,1)}), bf16[16,2,32768]{2,1,0:T(2,128)(2,1)S(1)}, u32[]{:S(2)}, u32[]{:S(2)}) async-start(bf16[16,2,32768]{2,1,0:T(2,128)(2,1)} %reshape.239), calls=%async_computation.1 | async-start | bytes 4194304 | tf_op jit(solution)/shard_map/all_to_all | solution.py:92
  419.0 7.8 %copy-start.5 = (bf16[1,256,4096]{1,2,0:T(8,128)(2,1)S(1)}, bf16[1,256,4096]{1,2,0:T(8,128)(2,1)}, u32[]{:S(2)}) copy-start(bf16[1,256,4096]{1,2,0:T(8,128)(2,1)} %copy.92) | copy-start | bytes 6291460
Sparse Core Ops, SparseCore 0:
  10.5 129.6 all-gather.1
where the time goes:
time: 460 us; the launch traced here: 455 us
  matrix products  192 us (42%)
  local copies, waits for them, and re-layouts  145 us (32%)
  other arithmetic  54 us (12%)
  waiting for transfers between devices  35.7 us (8%)
  starting transfers between devices  14.2 us (3%)
  between operations  14 us (3%)
    dot_general x16, matrix products, close_einsum(): return jnp.einsum(form, left, right, precision=lax.Precision.HIGH)  139 us
    another operation x7, local copies, waits for them, and re-layouts  61.1 us
    unnamed x6, other arithmetic  43.1 us
    unnamed x38, local copies, waits for them, and re-layouts  32.1 us
    all_to_all x1, waiting for transfers between devices, on_device(): lax.all_to_all(mixed, 'ctx', split_axis=1, concat_axis=2, tiled=True)  25.9 us
    dot_general x2, matrix products, split_einsum(): jnp.einsum(form, table_high, signal, preferred_element_type=jnp.float32)  25.3 us
    convert_element_type x1, local copies, waits for them, and re-layouts, on_device(): mixed = (causal + local_skip[None, None, :] * signal).astype(jnp.bfloat16)  25.3 us
    dot_general x1, matrix products, on_device(): jnp.dot(tok_rows, lax.all_gather(out_weight, ('dp', 'ctx'), axis=1, tiled...  16.9 us
  transfers between devices with their start and end apart: 3, of which 2 were waited for; matrix products, arithmetic and copies ran while one was open for 82% of the time, Pallas kernels for 0%

commit v1 on v0

--- a/solution.py
+++ b/solution.py
@@ -81,7 +81,10 @@
     response = filters.T.reshape(1, half, 128, channels)
     filt_re, filt_im = forward(response)
     local_skip = lax.dynamic_slice_in_dim(skip_gain, lax.axis_index("ctx") * channels, channels)
-    piece = lax.all_to_all(product, "ctx", split_axis=2, concat_axis=1, tiled=True)
+    piece = jnp.concatenate(
+        lax.all_to_all(jnp.stack(jnp.split(product, lax.axis_size("ctx"), axis=2)), "ctx", 0, 0),
+        axis=1,
+    )
     count = piece.shape[0]
     signal = piece.astype(jnp.float32)
     spec_re, spec_im = forward(piece.reshape(count, half, 128, channels))

time: 460 us -> 420 us (0.913)
  blocking collectives: 0 us -> 31.7 us
  waiting for transfers between devices: 35.7 us -> 4.72 us
  other arithmetic: 54 us -> 32.2 us
  local copies, waits for them, and re-layouts: 145 us -> 127 us
  starting transfers between devices: 14.2 us -> 7.96 us
    all_to_all x0 -> x1, blocking collectives: none -> 31.7 us  [on_device(): lax.all_to_all(mixed, 'ctx', split_axis=1, concat_axis=2, tiled=True)]
    all_to_all x2 -> x1, waiting for transfers between devices: 35 us -> 4.01 us  [on_device(): lax.all_to_all(jnp.stack(jnp.split(product, lax.axis_size('ctx'), axis=2)...]
    unnamed x6 -> x5, other arithmetic: 43.1 us -> 21.6 us
    convert_element_type x2 -> x0, local copies, waits for them, and re-layouts: 11.9 us -> none  [the longest x1 7.3 us: on_device(): (keys_in.astype(jnp.float32) * values_in.astype(jnp.float32)).astype(jnp....]
    unnamed x38 -> x47, local copies, waits for them, and re-layouts: 32.1 us -> 25.3 us
    all_to_all x2 -> x1, starting transfers between devices: 14.2 us -> 7.96 us  [on_device(): lax.all_to_all(jnp.stack(jnp.split(product, lax.axis_size('ctx'), axis=2)...]
    all_to_all x2 -> x0, local copies, waits for them, and re-layouts: 5.44 us -> none  [the longest x1 2.9 us: on_device(): lax.all_to_all(product, 'ctx', split_axis=2, concat_axis=1, tiled=True)]
    convert_element_type x1 -> x2, local copies, waits for them, and re-layouts: 5.38 us -> 9.42 us  [on_device(): returned.astype(jnp.float32)]
  transfers between devices with their start and end apart: 3 -> 2, of which waited for: 2 -> 1; matrix products, arithmetic and copies ran while one was open for 82% -> 81% of each run, Pallas kernels for 0% -> 0%
where the time goes in v1:
time: 420 us; the launch traced here: 413 us
  matrix products  195 us (46%)
  local copies, waits for them, and re-layouts  127 us (30%)
  other arithmetic  32.2 us (8%)
  blocking collectives  31.7 us (8%)
  between operations  13.8 us (3%)
  starting transfers between devices  7.96 us (2%)
  waiting for transfers between devices  4.72 us (1%)
    dot_general x16, matrix products, close_einsum(): return jnp.einsum(form, left, right, precision=lax.Precision.HIGH)  139 us
    another operation x7, local copies, waits for them, and re-layouts  62 us
    all_to_all x1, blocking collectives, on_device(): lax.all_to_all(mixed, 'ctx', split_axis=1, concat_axis=2, tiled=True)  31.7 us
    dot_general x2, matrix products, split_einsum(): jnp.einsum(form, table_high, signal, preferred_element_type=jnp.float32)  28.3 us
    unnamed x47, local copies, waits for them, and re-layouts  25.3 us
    convert_element_type x1, local copies, waits for them, and re-layouts, on_device(): mixed = (causal + local_skip[None, None, :] * signal).astype(jnp.bfloat16)  25.2 us
    unnamed x5, other arithmetic  21.6 us
    dot_general x1, matrix products, on_device(): jnp.dot(tok_rows, lax.all_gather(out_weight, ('dp', 'ctx'), axis=1, tiled...  17.6 us
  transfers between devices with their start and end apart: 2, of which 1 were waited for; matrix products, arithmetic and copies ran while one was open for 81% of the time, Pallas kernels for 0%

profile of v1, /device:TPU:0, one launch (start us, length us, event | category | flops | bytes accessed | tf_op | source)
XLA Modules:
  0.0 412.5 jit_solution(17861088934794895559)
XLA Ops:
  21.0 8.0 %all-to-all-start = ((bf16[16,1,256,256]{3,2,1,0:T(8,128)(2,1)}), bf16[16,1,256,256]{3,2,1,0:T(8,128)(2,1)S(1)}, u32[]{:S(2)}, u32[]{:S(2)}) async-start(bf16[16,1,256,256]{3,2,1,0:T(8,128)(2,1)} %fusion.32), calls=%async_computation | async-start | bytes 4194304 | tf_op jit(solution)/shard_map/all_to_all | solution.py:85
  41.6 8.9 %fusion.102 = f32[64,128,256]{2,0,1:T(8,128)} fusion(f32[32,128,256]{2,0,1:T(8,128)} %copy.86), kind=kOutput, calls=%fused_computation.135 | convolution fusion | flops 402681856 | bytes 12582912 | tf_op jit(solution)/shard_map/kn,snbc->skbc/dot_general | solution.py:19
  50.5 6.5 %fusion.98 = f32[64,128,256]{2,0,1:T(8,128)} fusion(f32[32,128,256]{2,0,1:T(8,128)S(1)} %copy-done.2), kind=kOutput, calls=%fused_computation.131 | convolution fusion | flops 402681856 | bytes 12582912 | tf_op jit(solution)/shard_map/kn,snbc->skbc/dot_general | solution.py:19
  73.2 26.8 %fusion.17 = (f32[64,128,256]{2,0,1:T(8,128)}, f32[64,128,256]{2,0,1:T(8,128)}, f32[64,128,256]{2,0,1:T(8,128)}, f32[64,128,256]{2,0,1:T(8,128)}) fusion(f32[128,256,64]{1,2,0:T(8,128)} %add_negate_fusion, f32[64,128]{0,1:T(8,128)S(1)} %copy.83, f32[64,128]{0,1:T(8,128)S(1)} %copy.80, f32[128,256,64]{1,2,0:T(8,128)} %fusion.28, ...), kind=kOutput, calls=%fused_computation.27 | convolution fusion | flops 163577856 | bytes 69275648 | tf_op jit(solution)/shard_map/kn,snbc->skbc/dot_general | solution.py:25
  100.0 9.6 %copy.88 = f32[64,128,256]{1,2,0:T(8,128)} copy(f32[64,128,256]{2,0,1:T(8,128)} %get-tuple-element.14) | data formatting | bytes 16777216 | tf_op jit(solution)/shard_map/reshape.25
  109.6 9.4 %copy.84 = f32[64,128,256]{1,2,0:T(8,128)} copy(f32[64,128,256]{2,0,1:T(8,128)} %get-tuple-element.9) | data formatting | bytes 16777216 | tf_op jit(solution)/shard_map/reshape.15
  119.0 9.6 %copy.89 = f32[64,128,256]{1,2,0:T(8,128)} copy(f32[64,128,256]{2,0,1:T(8,128)} %get-tuple-element.13) | data formatting | bytes 16777216 | tf_op jit(solution)/shard_map/reshape.27
  128.6 9.3 %copy.85 = f32[64,128,256]{1,2,0:T(8,128)} copy(f32[64,128,256]{2,0,1:T(8,128)} %get-tuple-element.10) | data formatting | bytes 16777216 | tf_op jit(solution)/shard_map/reshape.19
  137.9 8.7 %fusion.59 = f32[64,256,128]{2,1,0:T(8,128)} fusion(f32[64,128,256]{1,2,0:T(8,128)} %copy.85), kind=kOutput, calls=%fused_computation.98 | convolution fusion | flops 1610842112 | bytes 16777216 | tf_op jit(solution)/shard_map/hb,skbc->skhc/dot_general | solution.py:19
  146.6 6.3 %fusion.65 = f32[64,256,128]{2,1,0:T(8,128)} fusion(f32[64,128,256]{1,2,0:T(8,128)S(1)} %copy-done.1), kind=kOutput, calls=%fused_computation.104 | convolution fusion | flops 1610842112 | bytes 16777216 | tf_op jit(solution)/shard_map/hb,skbc->skhc/dot_general | solution.py:19
  152.9 6.2 %fusion.53 = f32[64,256,128]{2,1,0:T(8,128)} fusion(f32[64,128,256]{1,2,0:T(8,128)S(1)} %bitcast.269), kind=kOutput, calls=%fused_computation.92 | convolution fusion | flops 1610842112 | bytes 16777216 | tf_op jit(solution)/shard_map/hb,skbc->skhc/dot_general | solution.py:19
  171.3 6.1 %fusion.69 = f32[64,256,128]{2,1,0:T(8,128)} fusion(f32[64,128,256]{1,2,0:T(8,128)S(1)} %bitcast.267), kind=kOutput, calls=%fused_computation.108 | convolution fusion | flops 1610842112 | bytes 16777216 | tf_op jit(solution)/shard_map/hb,skbc->skhc/dot_general | solution.py:19
  177.4 6.4 %fusion.57 = f32[64,256,128]{2,1,0:T(8,128)} fusion(f32[64,128,256]{1,2,0:T(8,128)S(1)} %bitcast.263), kind=kOutput, calls=%fused_computation.96 | convolution fusion | flops 1610842112 | bytes 16777216 | tf_op jit(solution)/shard_map/hb,skbc->skhc/dot_general | solution.py:19
  183.8 29.1 %multiply_subtract_fusion = (f32[64,256,128]{2,1,0:T(8,128)}, f32[64,256,128]{2,1,0:T(8,128)}) fusion(f32[64,256,128]{2,1,0:T(8,128)} %fusion.53, f32[64,256,128]{2,1,0:T(8,128)} %fusion.65, f32[64,256,128]{2,1,0:T(8,128)} %fusion.55, f32[64,256,128]{2,1,0:T(8,128)} %fusion.67, f32[64,256,128]{2,1,0:T(8,128)} %fusion.57, f32[64,256,128]{2,1,0:T(8,128)} %fusion.69, ...), kind=kOutput, calls=%fused_computation.33 | convolution fusion | flops 1631813632 | bytes 83886080 | tf_op jit(solution)/shard_map/hb,skbc->skhc/dot_general | solution.py:19
  212.9 8.7 %fusion.4 = f32[64,256,128]{2,1,0:T(8,128)} fusion(f32[64,256,128]{2,1,0:T(8,128)} %get-tuple-element.5), kind=kOutput, calls=%fused_computation.6 | convolution fusion | flops 1610842112 | bytes 16777216 | tf_op jit(solution)/shard_map/hb,skhc->skbc/dot_general | solution.py:19
  233.7 19.7 %fusion.3 = (f32[64,128,256]{1,2,0:T(8,128)}, f32[64,128,256]{1,2,0:T(8,128)}) fusion(f32[64,128]{1,0:T(8,128)S(1)} %get-tuple-element.15, f32[64,128]{1,0:T(8,128)S(1)} %get-tuple-element.16, f32[64,256,128]{2,1,0:T(8,128)} %fusion.8, f32[64,256,128]{2,1,0:T(8,128)} %fusion.4, f32[64,256,128]{2,1,0:T(8,128)} %fusion.6, f32[64,256,128]{2,1,0:T(8,128)} %get-tuple-element.6), kind=kOutput, calls=%fused_computation.5 | convolution fusion | flops 1627619328 | bytes 50397184 | tf_op jit(solution)/shard_map/hb,skhc->skbc/dot_general | solution.py:19
  253.5 9.2 %copy.94 = f32[64,128,256]{2,0,1:T(8,128)} copy(f32[64,128,256]{1,2,0:T(8,128)} %get-tuple-element.8) | data formatting | bytes 16777216 | tf_op jit(solution)/shard_map/reshape.45
  262.7 9.2 %copy.95 = f32[64,128,256]{2,0,1:T(8,128)} copy(f32[64,128,256]{1,2,0:T(8,128)} %get-tuple-element.7) | data formatting | bytes 16777216 | tf_op jit(solution)/shard_map/reshape.47
  284.0 25.2 %copy.111 = bf16[1,4096,256]{2,0,1:T(2,128)(2,1)} copy(bf16[1,4096,256]{2,1,0:T(8,128)(2,1)S(1)} %fusion.22) | data formatting | bytes 4194304 | tf_op jit(solution)/shard_map/convert_element_type | solution.py:94
  309.8 21.6 %reduce = bf16[4096,256]{1,0:T(8,128)(2,1)S(1)} reduce(bf16[4096,1,256]{2,1,0:T(2,128)(2,1)} %bitcast.275, bf16[]{:T(256)} %broadcast.280), dimensions={1}, to_apply=%bitcast.261.reduce_sub_computation | reduce | bytes 4194306
  333.4 31.7 %all_to_all.14 = bf16[16,2,32768]{2,1,0:T(2,128)(2,1)S(1)} all-to-all(bf16[16,2,32768]{2,1,0:T(2,128)(2,1)} %reshape.236), channel_id=1, replica_groups=mesh['dp'=8,'ctx'=16] {'ctx'}, dimensions={0} | all-to-all | bytes 4194304 | tf_op jit(solution)/shard_map/all_to_all | solution.py:95
  365.1 6.8 %reshape.237 = bf16[4096,1,256]{2,1,0:T(2,128)(2,1)} reshape(bf16[16,2,32768]{2,1,0:T(2,128)(2,1)S(1)} %all_to_all.14) | data formatting | bytes 4194304
  371.9 6.5 %convert_bitcast_fusion = f32[1,256,16,256]{3,0,1,2:T(1,128)S(1)} fusion(bf16[1,16,256,256]{3,0,2,1:T(2,128)(2,1)} %bitcast.276), kind=kLoop, calls=%fused_computation.37 | loop fusion | flops 1048576 | bytes 6291456 | tf_op jit(solution)/shard_map/convert_element_type | solution.py:96
  387.8 17.6 %fusion.20 = bf16[1,256,4096]{2,1,0:T(8,128)(2,1)} fusion(bf16[4096,4096]{0,1:T(8,128)(2,1)} %all-gather.2.cloned.1.call-done, f32[1,256,4096]{2,1,0:T(8,128)} %reshape.226, bf16[1,256,4096]{2,1,0:T(8,128)(2,1)S(1)} %copy-done.5), kind=kOutput, calls=%fused_computation.36 | convolution fusion | flops 8594128896 | bytes 41943040 | tf_op jit(solution)/shard_map/dot_general | solution.py:99
  (76 shorter events, 91.7 us)
Async XLA Ops:
  6.5 381.3 %all-gather.2.cloned.1.call-start = ((), (), s32[]{:S(2)}) async-start(), calls=%async_computation.2 | async-start | bytes 33816576 | tf_op jit(solution)/shard_map/all_gather | solution.py:101
  21.0 40.0 %all-to-all-start = ((bf16[16,1,256,256]{3,2,1,0:T(8,128)(2,1)}), bf16[16,1,256,256]{3,2,1,0:T(8,128)(2,1)S(1)}, u32[]{:S(2)}, u32[]{:S(2)}) async-start(bf16[16,1,256,256]{3,2,1,0:T(8,128)(2,1)} %fusion.32), calls=%async_computation | async-start | bytes 4194304 | tf_op jit(solution)/shard_map/all_to_all | solution.py:85
  40.1 10.4 %copy-start.2 = (f32[32,128,256]{2,0,1:T(8,128)S(1)}, f32[32,128,256]{2,0,1:T(8,128)}, u32[]{:S(2)}) copy-start(f32[32,128,256]{2,0,1:T(8,128)} %copy.86) | copy-start | bytes 12582916
  137.9 8.7 %copy-start.1 = (f32[64,128,256]{1,2,0:T(8,128)S(1)}, f32[64,128,256]{1,2,0:T(8,128)}, u32[]{:S(2)}) copy-start(f32[64,128,256]{1,2,0:T(8,128)} %copy.85) | copy-start | bytes 25165828
  137.9 14.9 %slice-start.6 = ((s8[8388608]{0:T(1024)(128)(4,1)}), s8[4194304]{0:T(1024)(128)(4,1)S(1)}, s32[]{:S(2)}) async-start(s8[8388608]{0:T(1024)(128)(4,1)} %bitcast.268), calls=%async_computation.9 | async-start | bytes 8388608
  146.6 6.3 %slice-start.7 = ((s8[8388608]{0:T(1024)(128)(4,1)}), s8[4194304]{0:T(1024)(128)(4,1)S(1)}, s32[]{:S(2)}) async-start(s8[8388608]{0:T(1024)(128)(4,1)} %bitcast.268), calls=%async_computation.10 | async-start | bytes 8388608
  152.9 12.3 %slice-start.4 = ((s8[8388608]{0:T(1024)(128)(4,1)}), s8[4194304]{0:T(1024)(128)(4,1)S(1)}, s32[]{:S(2)}) async-start(s8[8388608]{0:T(1024)(128)(4,1)} %bitcast.266), calls=%async_computation.7 | async-start | bytes 8388608
  159.1 6.1 %slice-start.5 = ((s8[8388608]{0:T(1024)(128)(4,1)}), s8[4194304]{0:T(1024)(128)(4,1)S(1)}, s32[]{:S(2)}) async-start(s8[8388608]{0:T(1024)(128)(4,1)} %bitcast.266), calls=%async_computation.8 | async-start | bytes 8388608
  165.2 12.2 %slice-start = ((s8[8388608]{0:T(1024)(128)(4,1)}), s8[4194304]{0:T(1024)(128)(4,1)S(1)}, s32[]{:S(2)}) async-start(s8[8388608]{0:T(1024)(128)(4,1)} %bitcast.262), calls=%async_computation.3 | async-start | bytes 8388608
  171.3 6.1 %slice-start.1 = ((s8[8388608]{0:T(1024)(128)(4,1)}), s8[4194304]{0:T(1024)(128)(4,1)S(1)}, s32[]{:S(2)}) async-start(s8[8388608]{0:T(1024)(128)(4,1)} %bitcast.262), calls=%async_computation.4 | async-start | bytes 8388608
  212.9 8.7 %copy-start = (f32[64,256,128]{2,1,0:T(8,128)S(1)}, f32[64,256,128]{2,1,0:T(8,128)}, u32[]{:S(2)}) copy-start(f32[64,256,128]{2,1,0:T(8,128)} %get-tuple-element.5) | copy-start | bytes 25165828
  212.9 14.8 %slice-start.2 = ((s8[8388608]{0:T(1024)(128)(4,1)}), s8[4194304]{0:T(1024)(128)(4,1)S(1)}, s32[]{:S(2)}) async-start(s8[8388608]{0:T(1024)(128)(4,1)} %bitcast.264), calls=%async_computation.5 | async-start | bytes 8388608
  221.5 6.1 %slice-start.3 = ((s8[8388608]{0:T(1024)(128)(4,1)}), s8[4194304]{0:T(1024)(128)(4,1)S(1)}, s32[]{:S(2)}) async-start(s8[8388608]{0:T(1024)(128)(4,1)} %bitcast.264), calls=%async_computation.6 | async-start | bytes 8388608
  271.9 5.8 %copy-start.3 = (f32[64,128,256]{2,0,1:T(8,128)S(1)}, f32[64,128,256]{2,0,1:T(8,128)}, u32[]{:S(2)}) copy-start(f32[64,128,256]{2,0,1:T(8,128)} %copy.95) | copy-start | bytes 25165828
  280.8 2.4 copy-start.4
  378.4 9.4 %copy-start.5 = (bf16[1,256,4096]{2,1,0:T(8,128)(2,1)S(1)}, bf16[1,256,4096]{2,1,0:T(8,128)(2,1)}, u32[]{:S(2)}) copy-start(bf16[1,256,4096]{2,1,0:T(8,128)(2,1)} %param.6) | copy-start | bytes 6291460
Sparse Core Ops, SparseCore 0:
  10.5 128.8 all-gather.1
